TPU v7x, 32 devices: a whole 2x2x4 slice. The times are simulated.
32 devices in a mesh: pts: 4 (over x, core), ctr: 8 (over z, y).
Axes of the slice: x: 2, y: 2, z: 4, core: 2. Of those that a mesh axis runs over, the one named last changes fastest.
Arguments:
- points: bfloat16 [32768, 128], P('pts'), may hold values from -16 to 16, as said below
- centers: bfloat16 [16384, 128], P('ctr'), may hold values from -16 to 16, as said below
- panel_inverse: bfloat16 [512, 512], P('pts'), as said below
- direction: float32 [32, 16384], P(None, 'ctr'), as said below
- residual: float32 [32, 16384], P(None, 'ctr'), as said below
Outputs:
- panel_rows: bfloat16 [16384, 512], P('ctr', 'pts')
- operator_image: float32 [32, 16384], P(None, 'ctr')
- new_residual: float32 [32, 16384], P(None, 'ctr')
Inputs may be any that keep to these rules, and one draw needn't show every extreme that they name: `points`: rows of 128 real features. `centers`: rows of 128 real features. panel_inverse is lower triangular with a positive diagonal. `direction`: finite real values. `residual`: finite real values.
All inputs are finite; a program needn't handle non-finite values.
Results may differ from a plain program's by a relative error of at most 0.001.
The roundings to bfloat16 on the way count: a program that leaves them out, or rounds other values in their place, can miss the bound.
Values may be sent and summed in bfloat16 or wider, within the bound.
A program may use at most 128 MiB of HBM per device.

v0:
```python
import math

import jax
import jax.numpy as jnp
from jax import lax
from jax.sharding import PartitionSpec as P

RIDGE_TERM = 0.002


def spread(value, axis, source):
    kept = jnp.where(lax.axis_index(axis) == source, value, 0).astype(value.dtype)
    return lax.psum(kept, axis)


def similarity(left, right):
    inner_terms = lax.dot_general(
        left, right, (((1,), (1,)), ((), ())), preferred_element_type=jnp.float32
    )
    left_sq = jnp.sum(jnp.square(left.astype(jnp.float32)), axis=1)
    right_sq = jnp.sum(jnp.square(right.astype(jnp.float32)), axis=1)
    feature_count = left.shape[1]
    return jnp.exp(
        -(left_sq[:, None] + right_sq[None, :] - 2.0 * inner_terms) / (2.0 * feature_count)
    )


def center_image(w_bf16, kernel_rows):
    return lax.psum(jnp.dot(w_bf16, kernel_rows, preferred_element_type=jnp.float32), "pts")


def shards(points, centers, panel_inverse, direction, residual):
    n_ctr = lax.axis_size("ctr")
    n_pts = lax.axis_size("pts")
    ctr_index = lax.axis_index("ctr")
    pts_index = lax.axis_index("pts")
    m_dev = centers.shape[0]
    npg = points.shape[0]
    panel_size = panel_inverse.shape[1]
    panel_share = panel_inverse.shape[0]
    outputs = direction.shape[0]
    contract_last = (((1,), (1,)), ((), ()))
    head_rows, head_vals = (
        spread(centers[:panel_size], "ctr", 0),
        spread(direction[:, :panel_size].astype(jnp.bfloat16), "ctr", 0),
    )
    z1_share = lax.dot_general(
        head_vals, panel_inverse, contract_last, preferred_element_type=jnp.float32
    ).astype(jnp.bfloat16)
    q_part = jnp.dot(z1_share, panel_inverse, preferred_element_type=jnp.float32)
    embedded = lax.dynamic_update_slice(
        jnp.zeros((outputs, panel_size), jnp.float32),
        z1_share.astype(jnp.float32),
        (jnp.int32(0), pts_index * panel_share),
    )
    q_sum, z1_full = lax.psum((q_part, embedded), "pts")
    q_bf16 = q_sum.astype(jnp.bfloat16)
    k_panel = similarity(centers, head_rows).astype(jnp.bfloat16)
    panel_rows = lax.dot_general(
        k_panel, panel_inverse, contract_last, preferred_element_type=jnp.float32
    ).astype(jnp.bfloat16)
    correction = lax.dot_general(q_bf16, k_panel, contract_last, preferred_element_type=jnp.float32)
    columns = ctr_index * m_dev + jnp.arange(m_dev, dtype=jnp.int32)
    padded = jnp.concatenate(
        [z1_full, jnp.zeros((outputs, m_dev - panel_size), jnp.float32)], axis=1
    )
    z_vector = jnp.where(columns[None, :] < panel_size, padded, direction - correction)
    z_bf16 = z_vector.astype(jnp.bfloat16)
    block_rows = min(512, npg)
    kernel_rows = lax.map(
        lambda point_rows: similarity(point_rows, centers).astype(jnp.bfloat16),
        points.reshape(npg // block_rows, block_rows, points.shape[1]),
    ).reshape(npg, m_dev)
    partial_value = lax.dot_general(
        z_bf16, kernel_rows, contract_last, preferred_element_type=jnp.float32
    )
    w_scale = 1.0 / (2.0 * math.sqrt(m_dev * n_ctr))
    image_scale = 1.0 / (2.0 * math.sqrt(npg * n_pts))
    pieces = npg // n_ctr
    w_full = lax.psum(partial_value, "ctr") * w_scale
    w_bf16 = w_full.astype(jnp.bfloat16)
    owned_w = lax.dynamic_slice_in_dim(w_full, ctr_index * pieces, pieces, 1)
    owned_bf16 = owned_w.astype(jnp.bfloat16)
    quarter = m_dev // n_pts
    z_part = lax.dynamic_slice_in_dim(z_vector, pts_index * quarter, quarter, 1)
    r_part = lax.dynamic_slice_in_dim(residual, pts_index * quarter, quarter, 1)
    w_squares, z_squares, r_squares = lax.psum(
        (
            jnp.sum(owned_w * owned_bf16.astype(jnp.float32), axis=1),
            jnp.sum(z_part * z_part, axis=1),
            jnp.sum(r_part * r_part, axis=1),
        ),
        ("pts", "ctr"),
    )
    center_terms = center_image(w_bf16, kernel_rows)
    operator_image = center_terms * image_scale + RIDGE_TERM * z_vector
    curvature = image_scale / w_scale * w_squares + RIDGE_TERM * z_squares
    new_residual = residual - (r_squares / curvature)[:, None] * operator_image
    return (panel_rows, operator_image, new_residual)


def solution(mesh):
    in_specs = (P("pts", None), P("ctr", None), P("pts", None), P(None, "ctr"), P(None, "ctr"))
    out_specs = (P("ctr", "pts"), P(None, "ctr"), P(None, "ctr"))
    return jax.shard_map(shards, mesh=mesh, in_specs=in_specs, out_specs=out_specs, check_vma=False)
```

profile of v0, /device:TPU:1, one launch (start us, length us, event | category | flops | bytes accessed | tf_op | source)
XLA Modules:
  0.0 319.6 jit_solution(15667040201595970454)
XLA Ops:
  7.2 1.6 slice_select_fusion
  8.9 0.8 fusion.14
  9.7 31.1 %psum.64 = bf16[32,512]{1,0:T(8,128)(2,1)S(1)} all-reduce(bf16[32,512]{1,0:T(8,128)(2,1)S(1)} %fusion.14), channel_id=1, replica_groups=mesh['pts'=4,'ctr'=8] {'ctr'}, use_global_device_ids=true, to_apply=%region_3.4 | all-reduce | flops 16384 | bytes 65536 | tf_op jit(solution)/shard_map/psum | solution.py:13
  41.7 1.4 multiply_reduce_fusion.2
  43.3 18.4 %psum.66 = bf16[32,512]{1,0:T(8,128)(2,1)S(1)} all-reduce(f32[32,512]{1,0:T(8,128)S(1)} %fusion.16), channel_id=1, replica_groups=mesh['pts'=4,'ctr'=8] {'pts'}, use_global_device_ids=true, to_apply=%region_5.6 | all-reduce | flops 16384 | bytes 98304 | tf_op jit(solution)/shard_map/psum | solution.py:56
  61.7 96.1 %while.10 = (s32[]{:T(128)}, bf16[16,512,2048]{2,1,0:T(8,128)(2,1)}, bf16[16,512,128]{2,1,0:T(8,128)(2,1)}, bf16[2048,128]{1,0:T(8,128)(2,1)}, s32[]{:T(128)}) while((s32[]{:T(128)}, bf16[16,512,2048]{2,1,0:T(8,128)(2,1)}, bf16[16,512,128]{2,1,0:T(8,128)(2,1)}, bf16[2048,128]{1,0:T(8,128)(2,1)}, s32[]{:T(128)}) %tuple.35), condition=%wide.region_9.10_spmd, body=%wide.region_6.9_spmd.sunk | while | flops 275707392 | bytes 3429449 | solution.py:70
  61.7 1.1 multiply_reduce_fusion.10
  62.8 1.4 multiply_reduce_fusion.9
  64.2 3.6 %fusion.35 = bf16[16,512,2048]{2,1,0:T(8,128)(2,1)} fusion(bf16[16,512,2048]{2,1,0:T(8,128)(2,1)} %get-tuple-element.72, s32[]{:T(128)S(6)} %copy.14, bf16[2048,128]{1,0:T(8,128)(2,1)} %get-tuple-element.79, f32[2048]{0:T(1024)S(1)} %multiply_reduce_fusion.9, f32[512]{0:T(512)S(1)} %multiply_reduce_fusion.10, bf16[16,512,128]{2,1,0:T(8,128)(2,1)} %get-tuple-element.78), kind=kOutput, calls=%fused_computation.2.clone.1 | convolution fusion | flops 274726912 | bytes 2763776 | tf_op jit(solution)/shard_map/while/body/eval_jaxpr/dot_general | solution.py:17
  67.8 1.0 multiply_reduce_fusion.10
  68.8 1.4 multiply_reduce_fusion.9
  70.2 3.5 %fusion.35 = bf16[16,512,2048]{2,1,0:T(8,128)(2,1)} fusion(bf16[16,512,2048]{2,1,0:T(8,128)(2,1)} %get-tuple-element.72, s32[]{:T(128)S(6)} %copy.14, bf16[2048,128]{1,0:T(8,128)(2,1)} %get-tuple-element.79, f32[2048]{0:T(1024)S(1)} %multiply_reduce_fusion.9, f32[512]{0:T(512)S(1)} %multiply_reduce_fusion.10, bf16[16,512,128]{2,1,0:T(8,128)(2,1)} %get-tuple-element.78), kind=kOutput, calls=%fused_computation.2.clone.1 | convolution fusion | flops 274726912 | bytes 2763776 | tf_op jit(solution)/shard_map/while/body/eval_jaxpr/dot_general | solution.py:17
  73.7 1.0 multiply_reduce_fusion.10
  74.8 1.4 multiply_reduce_fusion.9
  76.2 3.5 %fusion.35 = bf16[16,512,2048]{2,1,0:T(8,128)(2,1)} fusion(bf16[16,512,2048]{2,1,0:T(8,128)(2,1)} %get-tuple-element.72, s32[]{:T(128)S(6)} %copy.14, bf16[2048,128]{1,0:T(8,128)(2,1)} %get-tuple-element.79, f32[2048]{0:T(1024)S(1)} %multiply_reduce_fusion.9, f32[512]{0:T(512)S(1)} %multiply_reduce_fusion.10, bf16[16,512,128]{2,1,0:T(8,128)(2,1)} %get-tuple-element.78), kind=kOutput, calls=%fused_computation.2.clone.1 | convolution fusion | flops 274726912 | bytes 2763776 | tf_op jit(solution)/shard_map/while/body/eval_jaxpr/dot_general | solution.py:17
  79.7 1.0 multiply_reduce_fusion.10
  80.8 1.4 multiply_reduce_fusion.9
  82.2 3.6 %fusion.35 = bf16[16,512,2048]{2,1,0:T(8,128)(2,1)} fusion(bf16[16,512,2048]{2,1,0:T(8,128)(2,1)} %get-tuple-element.72, s32[]{:T(128)S(6)} %copy.14, bf16[2048,128]{1,0:T(8,128)(2,1)} %get-tuple-element.79, f32[2048]{0:T(1024)S(1)} %multiply_reduce_fusion.9, f32[512]{0:T(512)S(1)} %multiply_reduce_fusion.10, bf16[16,512,128]{2,1,0:T(8,128)(2,1)} %get-tuple-element.78), kind=kOutput, calls=%fused_computation.2.clone.1 | convolution fusion | flops 274726912 | bytes 2763776 | tf_op jit(solution)/shard_map/while/body/eval_jaxpr/dot_general | solution.py:17
  85.8 1.0 multiply_reduce_fusion.10
  86.8 1.4 multiply_reduce_fusion.9
  88.2 3.6 %fusion.35 = bf16[16,512,2048]{2,1,0:T(8,128)(2,1)} fusion(bf16[16,512,2048]{2,1,0:T(8,128)(2,1)} %get-tuple-element.72, s32[]{:T(128)S(6)} %copy.14, bf16[2048,128]{1,0:T(8,128)(2,1)} %get-tuple-element.79, f32[2048]{0:T(1024)S(1)} %multiply_reduce_fusion.9, f32[512]{0:T(512)S(1)} %multiply_reduce_fusion.10, bf16[16,512,128]{2,1,0:T(8,128)(2,1)} %get-tuple-element.78), kind=kOutput, calls=%fused_computation.2.clone.1 | convolution fusion | flops 274726912 | bytes 2763776 | tf_op jit(solution)/shard_map/while/body/eval_jaxpr/dot_general | solution.py:17
  91.8 1.1 multiply_reduce_fusion.10
  92.9 1.4 multiply_reduce_fusion.9
  94.3 3.5 %fusion.35 = bf16[16,512,2048]{2,1,0:T(8,128)(2,1)} fusion(bf16[16,512,2048]{2,1,0:T(8,128)(2,1)} %get-tuple-element.72, s32[]{:T(128)S(6)} %copy.14, bf16[2048,128]{1,0:T(8,128)(2,1)} %get-tuple-element.79, f32[2048]{0:T(1024)S(1)} %multiply_reduce_fusion.9, f32[512]{0:T(512)S(1)} %multiply_reduce_fusion.10, bf16[16,512,128]{2,1,0:T(8,128)(2,1)} %get-tuple-element.78), kind=kOutput, calls=%fused_computation.2.clone.1 | convolution fusion | flops 274726912 | bytes 2763776 | tf_op jit(solution)/shard_map/while/body/eval_jaxpr/dot_general | solution.py:17
  97.8 1.1 multiply_reduce_fusion.10
  98.8 1.4 multiply_reduce_fusion.9
  100.2 3.6 %fusion.35 = bf16[16,512,2048]{2,1,0:T(8,128)(2,1)} fusion(bf16[16,512,2048]{2,1,0:T(8,128)(2,1)} %get-tuple-element.72, s32[]{:T(128)S(6)} %copy.14, bf16[2048,128]{1,0:T(8,128)(2,1)} %get-tuple-element.79, f32[2048]{0:T(1024)S(1)} %multiply_reduce_fusion.9, f32[512]{0:T(512)S(1)} %multiply_reduce_fusion.10, bf16[16,512,128]{2,1,0:T(8,128)(2,1)} %get-tuple-element.78), kind=kOutput, calls=%fused_computation.2.clone.1 | convolution fusion | flops 274726912 | bytes 2763776 | tf_op jit(solution)/shard_map/while/body/eval_jaxpr/dot_general | solution.py:17
  103.8 1.0 multiply_reduce_fusion.10
  104.9 1.4 multiply_reduce_fusion.9
  106.3 3.6 %fusion.35 = bf16[16,512,2048]{2,1,0:T(8,128)(2,1)} fusion(bf16[16,512,2048]{2,1,0:T(8,128)(2,1)} %get-tuple-element.72, s32[]{:T(128)S(6)} %copy.14, bf16[2048,128]{1,0:T(8,128)(2,1)} %get-tuple-element.79, f32[2048]{0:T(1024)S(1)} %multiply_reduce_fusion.9, f32[512]{0:T(512)S(1)} %multiply_reduce_fusion.10, bf16[16,512,128]{2,1,0:T(8,128)(2,1)} %get-tuple-element.78), kind=kOutput, calls=%fused_computation.2.clone.1 | convolution fusion | flops 274726912 | bytes 2763776 | tf_op jit(solution)/shard_map/while/body/eval_jaxpr/dot_general | solution.py:17
  109.8 1.0 multiply_reduce_fusion.10
  110.9 1.4 multiply_reduce_fusion.9
  112.3 3.6 %fusion.35 = bf16[16,512,2048]{2,1,0:T(8,128)(2,1)} fusion(bf16[16,512,2048]{2,1,0:T(8,128)(2,1)} %get-tuple-element.72, s32[]{:T(128)S(6)} %copy.14, bf16[2048,128]{1,0:T(8,128)(2,1)} %get-tuple-element.79, f32[2048]{0:T(1024)S(1)} %multiply_reduce_fusion.9, f32[512]{0:T(512)S(1)} %multiply_reduce_fusion.10, bf16[16,512,128]{2,1,0:T(8,128)(2,1)} %get-tuple-element.78), kind=kOutput, calls=%fused_computation.2.clone.1 | convolution fusion | flops 274726912 | bytes 2763776 | tf_op jit(solution)/shard_map/while/body/eval_jaxpr/dot_general | solution.py:17
  115.8 1.0 multiply_reduce_fusion.10
  116.9 1.4 multiply_reduce_fusion.9
  118.3 3.5 %fusion.35 = bf16[16,512,2048]{2,1,0:T(8,128)(2,1)} fusion(bf16[16,512,2048]{2,1,0:T(8,128)(2,1)} %get-tuple-element.72, s32[]{:T(128)S(6)} %copy.14, bf16[2048,128]{1,0:T(8,128)(2,1)} %get-tuple-element.79, f32[2048]{0:T(1024)S(1)} %multiply_reduce_fusion.9, f32[512]{0:T(512)S(1)} %multiply_reduce_fusion.10, bf16[16,512,128]{2,1,0:T(8,128)(2,1)} %get-tuple-element.78), kind=kOutput, calls=%fused_computation.2.clone.1 | convolution fusion | flops 274726912 | bytes 2763776 | tf_op jit(solution)/shard_map/while/body/eval_jaxpr/dot_general | solution.py:17
  121.8 1.0 multiply_reduce_fusion.10
  122.8 1.4 multiply_reduce_fusion.9
  124.2 3.5 %fusion.35 = bf16[16,512,2048]{2,1,0:T(8,128)(2,1)} fusion(bf16[16,512,2048]{2,1,0:T(8,128)(2,1)} %get-tuple-element.72, s32[]{:T(128)S(6)} %copy.14, bf16[2048,128]{1,0:T(8,128)(2,1)} %get-tuple-element.79, f32[2048]{0:T(1024)S(1)} %multiply_reduce_fusion.9, f32[512]{0:T(512)S(1)} %multiply_reduce_fusion.10, bf16[16,512,128]{2,1,0:T(8,128)(2,1)} %get-tuple-element.78), kind=kOutput, calls=%fused_computation.2.clone.1 | convolution fusion | flops 274726912 | bytes 2763776 | tf_op jit(solution)/shard_map/while/body/eval_jaxpr/dot_general | solution.py:17
  127.8 1.0 multiply_reduce_fusion.10
  128.8 1.4 multiply_reduce_fusion.9
  130.2 3.6 %fusion.35 = bf16[16,512,2048]{2,1,0:T(8,128)(2,1)} fusion(bf16[16,512,2048]{2,1,0:T(8,128)(2,1)} %get-tuple-element.72, s32[]{:T(128)S(6)} %copy.14, bf16[2048,128]{1,0:T(8,128)(2,1)} %get-tuple-element.79, f32[2048]{0:T(1024)S(1)} %multiply_reduce_fusion.9, f32[512]{0:T(512)S(1)} %multiply_reduce_fusion.10, bf16[16,512,128]{2,1,0:T(8,128)(2,1)} %get-tuple-element.78), kind=kOutput, calls=%fused_computation.2.clone.1 | convolution fusion | flops 274726912 | bytes 2763776 | tf_op jit(solution)/shard_map/while/body/eval_jaxpr/dot_general | solution.py:17
  133.8 1.0 multiply_reduce_fusion.10
  134.8 1.4 multiply_reduce_fusion.9
  136.2 3.6 %fusion.35 = bf16[16,512,2048]{2,1,0:T(8,128)(2,1)} fusion(bf16[16,512,2048]{2,1,0:T(8,128)(2,1)} %get-tuple-element.72, s32[]{:T(128)S(6)} %copy.14, bf16[2048,128]{1,0:T(8,128)(2,1)} %get-tuple-element.79, f32[2048]{0:T(1024)S(1)} %multiply_reduce_fusion.9, f32[512]{0:T(512)S(1)} %multiply_reduce_fusion.10, bf16[16,512,128]{2,1,0:T(8,128)(2,1)} %get-tuple-element.78), kind=kOutput, calls=%fused_computation.2.clone.1 | convolution fusion | flops 274726912 | bytes 2763776 | tf_op jit(solution)/shard_map/while/body/eval_jaxpr/dot_general | solution.py:17
  139.8 1.0 multiply_reduce_fusion.10
  140.9 1.4 multiply_reduce_fusion.9
  142.3 3.5 %fusion.35 = bf16[16,512,2048]{2,1,0:T(8,128)(2,1)} fusion(bf16[16,512,2048]{2,1,0:T(8,128)(2,1)} %get-tuple-element.72, s32[]{:T(128)S(6)} %copy.14, bf16[2048,128]{1,0:T(8,128)(2,1)} %get-tuple-element.79, f32[2048]{0:T(1024)S(1)} %multiply_reduce_fusion.9, f32[512]{0:T(512)S(1)} %multiply_reduce_fusion.10, bf16[16,512,128]{2,1,0:T(8,128)(2,1)} %get-tuple-element.78), kind=kOutput, calls=%fused_computation.2.clone.1 | convolution fusion | flops 274726912 | bytes 2763776 | tf_op jit(solution)/shard_map/while/body/eval_jaxpr/dot_general | solution.py:17
  145.8 1.0 multiply_reduce_fusion.10
  146.9 1.4 multiply_reduce_fusion.9
  148.3 3.6 %fusion.35 = bf16[16,512,2048]{2,1,0:T(8,128)(2,1)} fusion(bf16[16,512,2048]{2,1,0:T(8,128)(2,1)} %get-tuple-element.72, s32[]{:T(128)S(6)} %copy.14, bf16[2048,128]{1,0:T(8,128)(2,1)} %get-tuple-element.79, f32[2048]{0:T(1024)S(1)} %multiply_reduce_fusion.9, f32[512]{0:T(512)S(1)} %multiply_reduce_fusion.10, bf16[16,512,128]{2,1,0:T(8,128)(2,1)} %get-tuple-element.78), kind=kOutput, calls=%fused_computation.2.clone.1 | convolution fusion | flops 274726912 | bytes 2763776 | tf_op jit(solution)/shard_map/while/body/eval_jaxpr/dot_general | solution.py:17
  151.8 1.0 multiply_reduce_fusion.10
  152.9 1.4 multiply_reduce_fusion.9
  154.3 3.5 %fusion.35 = bf16[16,512,2048]{2,1,0:T(8,128)(2,1)} fusion(bf16[16,512,2048]{2,1,0:T(8,128)(2,1)} %get-tuple-element.72, s32[]{:T(128)S(6)} %copy.14, bf16[2048,128]{1,0:T(8,128)(2,1)} %get-tuple-element.79, f32[2048]{0:T(1024)S(1)} %multiply_reduce_fusion.9, f32[512]{0:T(512)S(1)} %multiply_reduce_fusion.10, bf16[16,512,128]{2,1,0:T(8,128)(2,1)} %get-tuple-element.78), kind=kOutput, calls=%fused_computation.2.clone.1 | convolution fusion | flops 274726912 | bytes 2763776 | tf_op jit(solution)/shard_map/while/body/eval_jaxpr/dot_general | solution.py:17
  157.8 1.1 multiply_reduce_fusion.3
  158.9 2.2 fusion.8
  161.2 1.3 fusion.9
  162.5 15.6 %fusion.12 = f32[32,8192]{1,0:T(8,128)} fusion(bf16[8192,2048]{1,0:T(8,128)(2,1)} %bitcast.41, f32[32,2048]{1,0:T(8,128)S(1)} %fusion.9), kind=kOutput, calls=%fused_computation.25 | convolution fusion | flops 1073807360 | bytes 34865152 | tf_op jit(solution)/shard_map/dot_general | solution.py:74
  178.5 1.6 convolution_convert_fusion
  180.0 72.8 %all-reduce.11.cloned.1.call-done = f32[32,8192]{1,0:T(8,128)} async-done(((f32[32,8192]{1,0:T(8,128)}), f32[32,8192]{1,0:T(8,128)}) %all-reduce.11.cloned.1.call-update) | async-done | bytes 1048592 | tf_op jit(solution)/shard_map/psum | solution.py:80
  252.9 1.3 broadcast_multiply_fusion
  254.3 17.5 %fusion.10 = f32[32,2048]{1,0:T(8,128)} fusion(bf16[8192,2048]{1,0:T(8,128)(2,1)} %bitcast.42, f32[32,8192]{1,0:T(8,128)} %all-reduce.11.cloned.1.call-done), kind=kOutput, calls=%fused_computation.18 | convolution fusion | flops 1074266112 | bytes 34865152 | tf_op jit(solution)/shard_map/dot_general | solution.py:29
  271.8 39.5 %all-reduce.1 = (f32[32]{0:T(128)S(1)}, f32[32]{0:T(128)S(1)}, f32[32]{0:T(128)S(1)}) all-reduce(f32[32]{0:T(128)S(1)} %multiply_reduce_fusion.6, f32[32]{0:T(128)S(1)} %multiply_reduce_fusion.5, f32[32]{0:T(128)S(1)} %multiply_reduce_fusion.4), channel_id=1, replica_groups=mesh['pts'=4,'ctr'=8] {'pts','ctr'}, use_global_device_ids=true, to_apply=%region_13.14 | all-reduce | flops 96 | bytes 768 | tf_op jit(solution)/shard_map/psum | solution.py:87
  311.3 1.8 multiply_subtract_fusion
  (28 shorter events, 1.6 us)
Async XLA Ops:
  7.2 33.7 %copy-start = (bf16[128,512]{1,0:T(8,128)(2,1)S(1)}, bf16[128,512]{1,0:T(8,128)(2,1)}, u32[]{:S(2)}) copy-start(bf16[128,512]{1,0:T(8,128)(2,1)} %param.9) | copy-start | bytes 393220
  7.2 150.6 %all-reduce.7.cloned.1.call-start = ((), (), s32[]{:S(2)}) async-start(), calls=%async_computation | async-start | bytes 262144 | tf_op jit(solution)/shard_map/psum | solution.py:13
  8.8 152.3 %all-reduce.9.cloned.1.call-start = ((), (), s32[]{:S(2)}) async-start(), calls=%async_computation.1 | async-start | bytes 131072 | tf_op jit(solution)/shard_map/psum | solution.py:56
  41.0 0.7 copy-start.3
  41.7 211.2 %all-reduce.11.cloned.1.call-start = ((), (), s32[]{:S(2)}) async-start(), calls=%async_computation.2 | async-start | bytes 2097152 | tf_op jit(solution)/shard_map/psum | solution.py:80
  157.8 3.3 %copy-start.2 = (f32[32,2048]{1,0:T(8,128)S(1)}, f32[32,2048]{1,0:T(8,128)}, u32[]{:S(2)}) copy-start(f32[32,2048]{1,0:T(8,128)} %param.10) | copy-start | bytes 786436
  162.5 15.7 %copy-start.1 = (f32[32,2048]{1,0:T(8,128)S(1)}, f32[32,2048]{1,0:T(8,128)}, u32[]{:S(2)}) copy-start(f32[32,2048]{1,0:T(8,128)} %param.11) | copy-start | bytes 786436
  178.2 133.2 %all-reduce.13.cloned.1.call-start = ((), (), s32[]{:S(2)}) async-start(), calls=%async_computation.3 | async-start | bytes 524288 | tf_op jit(solution)/shard_map/psum | solution.py:29
Sparse Core Ops, SparseCore 0:
  11.9 69.9 all-reduce.6
  84.9 30.7 all-reduce.8
  178.3 74.5 all-reduce.10
  271.9 30.8 all-reduce.12
where the time goes:
time: 323 us; the launch traced here: 320 us
  matrix products  95.4 us (30%)
  blocking collectives  89.1 us (28%)
  waiting for transfers between devices  72.9 us (23%)
  other arithmetic  47.3 us (15%)
  between operations  13.9 us (4%)
    psum x1, waiting for transfers between devices, shards(): w_full = lax.psum(partial_value, 'ctr') * w_scale  72.8 us
    dot_general x17, matrix products, similarity(): lax.dot_general(left, right, (((1,), (1,)), ((), ())), preferred_element_...  59.1 us
    psum x1, blocking collectives, shards(): lax.psum((jnp.sum(owned_w * owned_bf16.astype(jnp.float32), axis=1), jnp....  39.5 us
    psum x1, blocking collectives, spread(): return lax.psum(kept, axis)  31.1 us
    reduce_sum x17, other arithmetic, similarity(): right_sq = jnp.sum(jnp.square(right.astype(jnp.float32)), axis=1)  23.3 us
    psum x1, blocking collectives, shards(): q_sum, z1_full = lax.psum((q_part, embedded), 'pts')  18.4 us
    reduce_sum x17, other arithmetic, similarity(): left_sq = jnp.sum(jnp.square(left.astype(jnp.float32)), axis=1)  18.2 us
    dot_general x1, matrix products, center_image(): jnp.dot(w_bf16, kernel_rows, preferred_element_type=jnp.float32)  17.5 us
  transfers between devices with their start and end apart: 4, of which 1 were waited for; matrix products, arithmetic and copies ran while one was open for 32% of the time, Pallas kernels for 0%

commit v1 on v0

v1 whole, which is shorter than its diff:
```python
import functools
import math

import jax
import jax.numpy as jnp
from jax import lax
from jax.experimental import pallas as pl
from jax.experimental.pallas import tpu as pltpu
from jax.sharding import PartitionSpec as P

RIDGE_TERM = 0.002
LINK = jnp.float32
NT = (((1,), (1,)), ((), ()))
F32 = jnp.float32
BF16 = jnp.bfloat16


def split_norms(rows):
    wide = rows.astype(F32)
    norms = jnp.sum(wide * wide, axis=1, keepdims=True)
    first = norms.astype(BF16).astype(F32)
    rest = norms - first
    second = rest.astype(BF16).astype(F32)
    return first, second, rest - second


def extended_left(rows):
    first, second, third = split_norms(rows)
    lane = lax.broadcasted_iota(jnp.int32, rows.shape, 1)
    ones = jnp.where(lane < 6, 1.0, 0.0)
    extra = jnp.where(
        lane == 0, first, jnp.where(lane == 1, second, jnp.where(lane == 2, third, ones))
    )
    return jnp.concatenate([rows, extra.astype(BF16)], axis=1)


def extended_right(rows):
    first, second, third = split_norms(rows)
    features = rows.shape[1]
    near, far = 1.0 / features, -0.5 / features
    lane = lax.broadcasted_iota(jnp.int32, rows.shape, 1)
    ones = jnp.where(lane < 3, far, 0.0)
    extra = jnp.where(
        lane == 3,
        first * far,
        jnp.where(lane == 4, second * far, jnp.where(lane == 5, third * far, ones)),
    )
    scaled = (rows.astype(F32) * near).astype(BF16)
    return jnp.concatenate([scaled, extra.astype(BF16)], axis=1)


def step(
    n_ctr, n_pts,
    points, centers, pinv, direction, residual,
    prow_out, image_out, resid_out,
    kmat, right_t, head_rows, head_vals, pfull, zvec, zlow,
    wsend, wrecv, wall, stat_send, stat_recv, img, irecv, oi, stat2_send, stat2_recv,
    head_sem, pin_send, pin_recv, w_send, w_recv, a_send, a_recv,
    s_send, s_recv, i_send, i_recv, o_send, o_recv, t_send, t_recv,
):
    ctr = lax.axis_index("ctr")
    pts = lax.axis_index("pts")
    m_dev, features = centers.shape
    npg = points.shape[0]
    share, panel = pinv.shape
    outputs = direction.shape[0]
    pieces = npg // n_ctr
    quarter = m_dev // n_pts
    w_scale = 1.0 / (2.0 * math.sqrt(m_dev * n_ctr))
    image_scale = 1.0 / (2.0 * math.sqrt(npg * n_pts))

    def ctr_peer(d):
        return lax.rem(ctr + d, n_ctr)

    def pts_peer(d):
        return lax.rem(pts + d, n_pts)

    def copy(src, dst, send_sem, recv_sem, axis, peer):
        return pltpu.make_async_remote_copy(
            src_ref=src, dst_ref=dst, send_sem=send_sem, recv_sem=recv_sem,
            device_id={axis: peer}, device_id_type=pl.DeviceIdType.MESH,
        )

    barrier = pltpu.get_barrier_semaphore()

    @pl.loop(1, n_ctr)
    def _(d):
        pl.semaphore_signal(
            barrier, inc=1, device_id={"ctr": ctr_peer(d)}, device_id_type=pl.DeviceIdType.MESH
        )

    @pl.loop(1, n_pts)
    def _(d):
        pl.semaphore_signal(
            barrier, inc=1, device_id={"pts": pts_peer(d)}, device_id_type=pl.DeviceIdType.MESH
        )

    pl.semaphore_wait(barrier, n_ctr + n_pts - 2)

    def vals_copy(peer):
        return copy(head_vals, head_vals, head_sem.at[0, peer], head_sem.at[2, 0], "ctr", peer)

    def rows_copy(peer):
        return copy(head_rows, head_rows, head_sem.at[1, peer], head_sem.at[3, 0], "ctr", peer)

    def pin_copy(slot, peer, recv_slot):
        return copy(pinv, pfull.at[slot], pin_send.at[peer], pin_recv.at[recv_slot], "pts", peer)

    @pl.when(ctr == 0)
    def _():
        head_vals[...] = direction[:, :panel].astype(BF16)
        head_rows[...] = centers[:panel, :]

        @pl.loop(1, n_ctr)
        def _(d):
            vals_copy(d).start()

        @pl.loop(1, n_ctr)
        def _(d):
            rows_copy(d).start()

    @pl.loop(1, n_pts)
    def _(d):
        pin_copy(pts, pts_peer(d), pts).start()

    pfull[pts] = pinv[...]

    tile_c = min(512, m_dev)
    for c in range(m_dev // tile_c):
        cols = slice(c * tile_c, (c + 1) * tile_c)
        right_t[:, cols] = extended_right(centers[cols, :]).astype(F32).T.astype(BF16)
    tile_p = min(256, npg)

    @pl.loop(0, npg // tile_p)
    def _(i):
        rows = pl.ds(pl.multiple_of(i * tile_p, tile_p), tile_p)
        left = extended_left(points[rows, :])
        for c in range(m_dev // tile_c):
            cols = slice(c * tile_c, (c + 1) * tile_c)
            kmat[rows, cols] = jnp.exp(
                jnp.dot(left, right_t[:, cols], preferred_element_type=F32)
            ).astype(BF16)

    @pl.when(ctr != 0)
    def _():
        vals_copy(0).wait_recv()
        rows_copy(0).wait_recv()

    @pl.loop(1, n_pts)
    def _(d):
        peer = pts_peer(d)
        pin_copy(peer, peer, peer).wait_recv()

    vals = head_vals[...]
    z1 = [
        lax.dot_general(vals, pfull[s], NT, preferred_element_type=F32).astype(BF16)
        for s in range(n_pts)
    ]
    q = sum(jnp.dot(z1[s], pfull[s], preferred_element_type=F32) for s in range(n_pts))
    q = q.astype(BF16)
    head_t = extended_right(head_rows[...]).astype(F32).T.astype(BF16)
    for c in range(m_dev // tile_c):
        cols = slice(c * tile_c, (c + 1) * tile_c)
        k_panel = jnp.exp(
            jnp.dot(extended_left(centers[cols, :]), head_t, preferred_element_type=F32)
        ).astype(BF16)
        prow_out[cols, :] = lax.dot_general(
            k_panel, pinv[...], NT, preferred_element_type=F32
        ).astype(BF16)
        zvec[:, cols] = direction[:, cols] - lax.dot_general(
            q, k_panel, NT, preferred_element_type=F32
        )

    @pl.when(ctr == 0)
    def _():
        for s in range(n_pts):
            zvec[:, s * share : (s + 1) * share] = z1[s].astype(F32)

    zlow[...] = zvec[...].astype(BF16)

    def piece_rows(j):
        return pl.ds(pl.multiple_of(j * pieces, pieces), pieces)

    def partial(j):
        return lax.dot_general(
            zlow[...], kmat[piece_rows(j), :], NT, preferred_element_type=F32
        )

    def w_copy(j, slot):
        return copy(wsend.at[j], wrecv.at[slot], w_send.at[j], w_recv.at[slot], "ctr", j)

    @pl.loop(1, n_ctr)
    def _(d):
        j = ctr_peer(d)
        wsend[j] = partial(j).astype(LINK)
        w_copy(j, ctr).start()

    wrecv[ctr] = partial(ctr).astype(LINK)

    z_squares = jnp.sum(zvec[...] * zvec[...], axis=1, keepdims=True)
    r_squares = jnp.sum(residual[...] * residual[...], axis=1, keepdims=True)

    @pl.loop(1, n_ctr)
    def _(d):
        j = ctr_peer(n_ctr - d)
        w_copy(j, j).wait_recv()

    owned = lax.fori_loop(
        1, n_ctr, lambda s, total: total + wrecv[s].astype(F32), wrecv[0].astype(F32)
    ) * w_scale
    owned_low = owned.astype(BF16)
    wall[ctr] = owned_low

    def a_copy(slot, peer):
        return copy(wall.at[slot], wall.at[slot], a_send.at[peer], a_recv.at[slot], "ctr", peer)

    @pl.loop(1, n_ctr)
    def _(d):
        a_copy(ctr, ctr_peer(d)).start()

    w_squares = jnp.sum(owned * owned_low.astype(F32), axis=1, keepdims=True)
    lane = lax.broadcasted_iota(jnp.int32, stat_send.shape, 1)
    stat_send[...] = jnp.where(
        lane == 0, w_squares, jnp.where(lane == 1, z_squares, jnp.where(lane == 2, r_squares, 0.0))
    )
    stat_recv[ctr] = stat_send[...]

    def s_copy(slot, peer):
        return copy(stat_send, stat_recv.at[slot], s_send.at[peer], s_recv.at[slot], "ctr", peer)

    @pl.loop(1, n_ctr)
    def _(d):
        s_copy(ctr, ctr_peer(d)).start()

    img[...] = jnp.dot(owned_low, kmat[piece_rows(ctr), :], preferred_element_type=F32)

    @pl.loop(1, n_ctr)
    def _(d):
        j = ctr_peer(n_ctr - d)
        a_copy(j, j).wait_recv()
        img[...] += jnp.dot(wall[j], kmat[piece_rows(j), :], preferred_element_type=F32)

    def quarter_cols(p):
        return pl.ds(pl.multiple_of(p * quarter, quarter), quarter)

    def i_copy(p, slot):
        return copy(
            img.at[:, quarter_cols(p)], irecv.at[slot], i_send.at[p], i_recv.at[slot], "pts", p
        )

    @pl.loop(1, n_pts)
    def _(d):
        i_copy(pts_peer(d), pts).start()

    @pl.loop(1, n_ctr)
    def _(d):
        j = ctr_peer(n_ctr - d)
        s_copy(j, j).wait_recv()

    stat_sum = lax.fori_loop(1, n_ctr, lambda s, total: total + stat_recv[s], stat_recv[0])
    stat2_send[...] = stat_sum
    stat2_recv[pts] = stat_sum

    def t_copy(slot, peer):
        return copy(stat2_send, stat2_recv.at[slot], t_send.at[peer], t_recv.at[slot], "pts", peer)

    @pl.loop(1, n_pts)
    def _(d):
        t_copy(pts, pts_peer(d)).start()

    irecv[pts] = img[:, quarter_cols(pts)]

    @pl.loop(1, n_pts)
    def _(d):
        j = pts_peer(d)
        i_copy(j, j).wait_recv()

    terms = irecv[0]
    for s in range(1, n_pts):
        terms = terms + irecv[s]
    oi[pts] = terms * image_scale + RIDGE_TERM * zvec[:, quarter_cols(pts)]

    def o_copy(slot, peer):
        return copy(oi.at[slot], oi.at[slot], o_send.at[peer], o_recv.at[slot], "pts", peer)

    @pl.loop(1, n_pts)
    def _(d):
        o_copy(pts, pts_peer(d)).start()

    @pl.loop(1, n_pts)
    def _(d):
        j = pts_peer(d)
        t_copy(j, j).wait_recv()

    w_total = stat2_recv[0][:, 0:1]
    for s in range(1, n_pts):
        w_total = w_total + stat2_recv[s][:, 0:1]
    curvature = image_scale / w_scale * w_total + RIDGE_TERM * stat_sum[:, 1:2]
    length = stat_sum[:, 2:3] / curvature

    @pl.loop(1, n_pts)
    def _(d):
        j = pts_peer(d)
        o_copy(j, j).wait_recv()

    for s in range(n_pts):
        cols = slice(s * quarter, (s + 1) * quarter)
        image_out[:, cols] = oi[s]
        resid_out[:, cols] = residual[:, cols] - length * oi[s]

    @pl.when(ctr == 0)
    def _():
        @pl.loop(1, n_ctr)
        def _(d):
            vals_copy(d).wait_send()
            rows_copy(d).wait_send()

    @pl.loop(1, n_ctr)
    def _(d):
        j = ctr_peer(d)
        w_copy(j, ctr).wait_send()
        a_copy(ctr, j).wait_send()
        s_copy(ctr, j).wait_send()

    @pl.loop(1, n_pts)
    def _(d):
        p = pts_peer(d)
        pin_copy(pts, p, pts).wait_send()
        i_copy(p, pts).wait_send()
        t_copy(pts, p).wait_send()
        o_copy(pts, p).wait_send()


def shards(n_ctr, n_pts, points, centers, panel_inverse, direction, residual):
    m_dev, features = centers.shape
    npg = points.shape[0]
    share, panel = panel_inverse.shape
    outputs = direction.shape[0]
    pieces = npg // n_ctr
    quarter = m_dev // n_pts
    vmem = pl.BlockSpec(memory_space=pltpu.VMEM)
    ctr_sem = pltpu.SemaphoreType.DMA((n_ctr,))
    pts_sem = pltpu.SemaphoreType.DMA((n_pts,))
    return pl.pallas_call(
        functools.partial(step, n_ctr, n_pts),
        out_shape=(
            jax.ShapeDtypeStruct((m_dev, share), BF16),
            jax.ShapeDtypeStruct((outputs, m_dev), F32),
            jax.ShapeDtypeStruct((outputs, m_dev), F32),
        ),
        in_specs=[vmem] * 5,
        out_specs=(vmem,) * 3,
        scratch_shapes=[
            pltpu.VMEM((npg, m_dev), BF16),
            pltpu.VMEM((2 * features, m_dev), BF16),
            pltpu.VMEM((panel, features), BF16),
            pltpu.VMEM((outputs, panel), BF16),
            pltpu.VMEM((n_pts, share, panel), BF16),
            pltpu.VMEM((outputs, m_dev), F32),
            pltpu.VMEM((outputs, m_dev), BF16),
            pltpu.VMEM((n_ctr, outputs, pieces), LINK),
            pltpu.VMEM((n_ctr, outputs, pieces), LINK),
            pltpu.VMEM((n_ctr, outputs, pieces), BF16),
            pltpu.VMEM((outputs, 128), F32),
            pltpu.VMEM((n_ctr, outputs, 128), F32),
            pltpu.VMEM((outputs, m_dev), F32),
            pltpu.VMEM((n_pts, outputs, quarter), F32),
            pltpu.VMEM((n_pts, outputs, quarter), F32),
            pltpu.VMEM((outputs, 128), F32),
            pltpu.VMEM((n_pts, outputs, 128), F32),
            pltpu.SemaphoreType.DMA((4, n_ctr)),
            pts_sem, pts_sem, ctr_sem, ctr_sem, ctr_sem, ctr_sem,
            ctr_sem, ctr_sem, pts_sem, pts_sem, pts_sem, pts_sem, pts_sem, pts_sem,
        ],
        compiler_params=pltpu.CompilerParams(
            collective_id=0, has_side_effects=True, vmem_limit_bytes=56 * 1024 * 1024
        ),
        cost_estimate=pl.CostEstimate(
            flops=2 * npg * m_dev * (2 * features + 2 * outputs),
            bytes_accessed=4 * npg * features,
            transcendentals=npg * m_dev,
        ),
    )(points, centers, panel_inverse, direction, residual)


def solution(mesh):
    n_ctr, n_pts = mesh.shape["ctr"], mesh.shape["pts"]
    in_specs = (P("pts", None), P("ctr", None), P("pts", None), P(None, "ctr"), P(None, "ctr"))
    out_specs = (P("ctr", "pts"), P(None, "ctr"), P(None, "ctr"))
    return jax.shard_map(
        functools.partial(shards, n_ctr, n_pts),
        mesh=mesh, in_specs=in_specs, out_specs=out_specs, check_vma=False,
    )
```

time: 323 us -> 89.9 us (0.28)
  matrix products: 95.4 us -> 0 us
  blocking collectives: 89.1 us -> 0 us
  Pallas kernels: 0 us -> 83.8 us
  waiting for transfers between devices: 72.9 us -> 0 us
  other arithmetic: 47.3 us -> 0 us
  between operations: 13.9 us -> 0.64 us
  local copies, waits for them, and re-layouts: 0.68 us -> 5.21 us
    dot_general x23 -> x0, matrix products: 95.4 us -> none  [the longest x17 59.1 us: similarity(): lax.dot_general(left, right, (((1,), (1,)), ((), ())), preferred_element_...]
    psum x3 -> x0, blocking collectives: 89.1 us -> none  [the longest x1 39.5 us: shards(): lax.psum((jnp.sum(owned_w * owned_bf16.astype(jnp.float32), axis=1), jnp....]
    pallas_call x0 -> x1, Pallas kernels: none -> 83.8 us  [shards(): pl.pallas_call(functools.partial(step, n_ctr, n_pts), out_shape=(jax.Shap...]
    psum x4 -> x0, waiting for transfers between devices: 72.9 us -> none  [the longest x1 72.8 us: shards(): w_full = lax.psum(partial_value, 'ctr') * w_scale]
    reduce_sum x37 -> x0, other arithmetic: 41.8 us -> none  [the longest x17 23.3 us: similarity(): right_sq = jnp.sum(jnp.square(right.astype(jnp.float32)), axis=1)]
    unnamed x8 -> x3, local copies, waits for them, and re-layouts: 0.67 us -> 5.21 us
  transfers between devices with their start and end apart: 4 -> 0, of which waited for: 1 -> 0; matrix products, arithmetic and copies ran while one was open for 32% -> 0% of each run, Pallas kernels for 0% -> 0%
where the time goes in v1:
time: 89.9 us; the launch traced here: 89.6 us
  Pallas kernels  83.8 us (93%)
  local copies, waits for them, and re-layouts  5.21 us (6%)
    pallas_call x1, Pallas kernels, shards(): pl.pallas_call(functools.partial(step, n_ctr, n_pts), out_shape=(jax.Shap...  83.8 us
    unnamed x3, local copies, waits for them, and re-layouts  5.21 us

profile of v1, /device:TPU:1, one launch (start us, length us, event | category | flops | bytes accessed | tf_op | source)
XLA Modules:
  0.0 89.6 jit_solution(8833080483295061391)
XLA Ops:
  0.6 83.8 %shard_map.76 = (bf16[2048,128]{1,0:T(8,128)(2,1)}, f32[32,2048]{1,0:T(8,128)}, f32[32,2048]{1,0:T(8,128)}) custom-call(bf16[8192,128]{1,0:T(8,128)(2,1)} %points.1, bf16[2048,128]{1,0:T(8,128)(2,1)} %centers.1, bf16[128,512]{1,0:T(8,128)(2,1)} %pinv.1, f32[32,2048]{1,0:T(8,128)} %direction.1, f32[32,2048]{1,0:T(8,128)} %residual.1), custom_call_target="tpu_custom_call" | custom-call | flops 10737418240 | bytes 4194304 | tf_op jit(solution)/shard_map/pallas_call | solution.py:344
  84.4 1.9 %copy.11 = bf16[2048,128]{1,0:T(8,128)(2,1)} copy(bf16[2048,128]{1,0:T(8,128)(2,1)} %get-tuple-element.6) | data formatting | bytes 1048576
  86.3 1.7 %copy.12 = f32[32,2048]{1,0:T(8,128)} copy(f32[32,2048]{1,0:T(8,128)} %get-tuple-element.7) | data formatting | bytes 524288
  88.0 1.7 %copy.13 = f32[32,2048]{1,0:T(8,128)} copy(f32[32,2048]{1,0:T(8,128)} %get-tuple-element.8) | data formatting | bytes 524288

commit v2 on v1

v2 whole, which is shorter than its diff:
```python
import functools
import math

import jax
import jax.numpy as jnp
from jax import lax
from jax.experimental import pallas as pl
from jax.experimental.pallas import tpu as pltpu
from jax.sharding import PartitionSpec as P

RIDGE_TERM = 0.002
NT = (((1,), (1,)), ((), ()))
F32 = jnp.float32
BF16 = jnp.bfloat16


def split_norms(rows):
    wide = rows.astype(F32)
    norms = jnp.sum(wide * wide, axis=1, keepdims=True)
    first = norms.astype(BF16).astype(F32)
    rest = norms - first
    second = rest.astype(BF16).astype(F32)
    return first, second, rest - second


def extended_left(rows):
    first, second, third = split_norms(rows)
    lane = lax.broadcasted_iota(jnp.int32, rows.shape, 1)
    ones = jnp.where(lane < 6, 1.0, 0.0)
    extra = jnp.where(
        lane == 0, first, jnp.where(lane == 1, second, jnp.where(lane == 2, third, ones))
    )
    return jnp.concatenate([rows, extra.astype(BF16)], axis=1)


def extended_right(rows):
    first, second, third = split_norms(rows)
    features = rows.shape[1]
    near, far = 1.0 / features, -0.5 / features
    lane = lax.broadcasted_iota(jnp.int32, rows.shape, 1)
    ones = jnp.where(lane < 3, far, 0.0)
    extra = jnp.where(
        lane == 3,
        first * far,
        jnp.where(lane == 4, second * far, jnp.where(lane == 5, third * far, ones)),
    )
    scaled = (rows.astype(F32) * near).astype(BF16)
    return jnp.concatenate([scaled, extra.astype(BF16)], axis=1)


def step(
    n_ctr, n_pts,
    points, centers, pinv, direction, residual,
    prow_out, image_out, resid_out,
    kmat, right_t, head_rows, head_vals, pfull, k_panel, zvec, zlow,
    ysend, yrecv, own, zrecv, wall, stat_send, stat_recv, img, irecv, oi, stat2_send, stat2_recv,
    h_send, h_recv, g_send, g_recv, pin_send, pin_recv, y_send, y_recv, z_send, z_recv,
    m_send, az_send, af_send, a_recv,
    s_send, s_recv, i_send, i_recv, o_send, o_recv, t_send, t_recv,
):
    ctr = lax.axis_index("ctr")
    pts = lax.axis_index("pts")
    m_dev, features = centers.shape
    npg = points.shape[0]
    share, panel = pinv.shape
    outputs = direction.shape[0]
    pieces = npg // n_ctr
    quarter = m_dev // n_pts
    half = n_ctr // 2
    side = lax.rem(ctr, 2)
    group = lax.div(ctr, 2)
    mate = 2 * group + 1 - side
    w_scale = 1.0 / (2.0 * math.sqrt(m_dev * n_ctr))
    image_scale = 1.0 / (2.0 * math.sqrt(npg * n_pts))

    def ctr_peer(d):
        return lax.rem(ctr + d, n_ctr)

    def pts_peer(d):
        return lax.rem(pts + d, n_pts)

    def group_at(d):
        return lax.rem(group + d, half)

    def copy(src, dst, send_sem, recv_sem, axis, peer):
        return pltpu.make_async_remote_copy(
            src_ref=src, dst_ref=dst, send_sem=send_sem, recv_sem=recv_sem,
            device_id={axis: peer}, device_id_type=pl.DeviceIdType.MESH,
        )

    barrier = pltpu.get_barrier_semaphore()

    @pl.loop(1, n_ctr)
    def _(d):
        pl.semaphore_signal(
            barrier, inc=1, device_id={"ctr": ctr_peer(d)}, device_id_type=pl.DeviceIdType.MESH
        )

    @pl.loop(1, n_pts)
    def _(d):
        pl.semaphore_signal(
            barrier, inc=1, device_id={"pts": pts_peer(d)}, device_id_type=pl.DeviceIdType.MESH
        )

    pl.semaphore_wait(barrier, n_ctr + n_pts - 2)

    def vals_copy(peer):
        return copy(
            head_vals.at[pts], head_vals.at[pts], h_send.at[0, peer], h_recv.at[0], "ctr", peer
        )

    def rows_copy(peer):
        return copy(
            head_rows.at[pts], head_rows.at[pts], h_send.at[1, peer], h_recv.at[1], "ctr", peer
        )

    def vals_pass(slot, peer):
        return copy(
            head_vals.at[slot], head_vals.at[slot], g_send.at[0, peer], g_recv.at[0, slot],
            "pts", peer,
        )

    def rows_pass(slot, peer):
        return copy(
            head_rows.at[slot], head_rows.at[slot], g_send.at[1, peer], g_recv.at[1, slot],
            "pts", peer,
        )

    def pin_copy(slot, peer):
        return copy(pinv, pfull.at[slot], pin_send.at[peer], pin_recv.at[slot], "pts", peer)

    @pl.when(ctr == 0)
    def _():
        part = pl.ds(pl.multiple_of(pts * share, share), share)
        head_vals[pts] = direction[:, part].astype(BF16)
        head_rows[pts] = centers[part, :]

        @pl.loop(1, n_ctr)
        def _(d):
            vals_copy(d).start()
            rows_copy(d).start()

    @pl.loop(1, n_pts)
    def _(d):
        pin_copy(pts, pts_peer(d)).start()

    pfull[pts] = pinv[...]

    tile_r = min(512, m_dev)
    for c in range(m_dev // tile_r):
        cols = slice(c * tile_r, (c + 1) * tile_r)
        right_t[:, cols] = extended_right(centers[cols, :]).astype(F32).T.astype(BF16)
    tile_p, tile_c = min(512, 2 * pieces), min(256, m_dev)

    def build(t):
        @pl.loop(0, 2 * pieces // tile_p)
        def _(i):
            rows = pl.ds(pl.multiple_of(t * 2 * pieces + i * tile_p, tile_p), tile_p)
            left = extended_left(points[rows, :])
            for c in range(m_dev // tile_c):
                cols = slice(c * tile_c, (c + 1) * tile_c)
                kmat[rows, cols] = jnp.exp(
                    jnp.dot(left, right_t[:, cols], preferred_element_type=F32)
                ).astype(BF16)

    early = half // 2
    first = early // 2

    @pl.loop(0, first)
    def _(k):
        build(group_at(k + 1))

    @pl.when(ctr != 0)
    def _():
        vals_copy(0).wait_recv()
        rows_copy(0).wait_recv()

    @pl.loop(1, n_pts)
    def _(d):
        vals_pass(pts, pts_peer(d)).start()
        rows_pass(pts, pts_peer(d)).start()

    @pl.loop(first, early)
    def _(k):
        build(group_at(k + 1))

    @pl.loop(1, n_pts)
    def _(d):
        peer = pts_peer(d)
        pin_copy(peer, peer).wait_recv()
        vals_pass(peer, peer).wait_recv()
        rows_pass(peer, peer).wait_recv()

    vals = jnp.concatenate([head_vals[s] for s in range(n_pts)], axis=1)
    z1 = [
        lax.dot_general(vals, pfull[s], NT, preferred_element_type=F32).astype(BF16)
        for s in range(n_pts)
    ]
    q = sum(jnp.dot(z1[s], pfull[s], preferred_element_type=F32) for s in range(n_pts))
    q = q.astype(BF16)
    head_t = jnp.concatenate(
        [extended_right(head_rows[s]).astype(F32).T.astype(BF16) for s in range(n_pts)], axis=1
    )
    for c in range(m_dev // tile_r):
        cols = slice(c * tile_r, (c + 1) * tile_r)
        k_tile = jnp.exp(
            jnp.dot(extended_left(centers[cols, :]), head_t, preferred_element_type=F32)
        ).astype(BF16)
        k_panel[cols, :] = k_tile
        zvec[:, cols] = direction[:, cols] - lax.dot_general(
            q, k_tile, NT, preferred_element_type=F32
        )

    @pl.when(ctr == 0)
    def _():
        for s in range(n_pts):
            zvec[:, s * share : (s + 1) * share] = z1[s].astype(F32)

    zlow[...] = zvec[...].astype(BF16)

    def piece_rows(j):
        return pl.ds(pl.multiple_of(j * pieces, pieces), pieces)

    def partial(j):
        return lax.dot_general(
            zlow[...], kmat[piece_rows(j), :], NT, preferred_element_type=F32
        )

    def y_copy(t):
        return copy(ysend.at[t], yrecv.at[t], y_send.at[t], y_recv.at[t], "ctr", mate)

    def z_copy(t, slot):
        return copy(own.at[t], zrecv.at[slot], z_send.at[t], z_recv.at[slot], "ctr", 2 * t + side)

    def product(t):
        ysend[t] = partial(2 * t + 1 - side)
        y_copy(t).start()
        own[t] = partial(2 * t + side)

    def pass_on(t):
        y_copy(t).wait_recv()
        own[t] = own[t] + yrecv[t]
        z_copy(t, group).start()

    @pl.loop(0, early)
    def _(k):
        product(group_at(k + 1))

        @pl.when(k > 0)
        def _():
            pass_on(group_at(k))

    @pl.loop(early, half)
    def _(k):
        build(group_at(k + 1))
        product(group_at(k + 1))

        @pl.when(k > 0)
        def _():
            pass_on(group_at(k))

    z_squares = jnp.sum(zvec[...] * zvec[...], axis=1, keepdims=True)
    r_squares = jnp.sum(residual[...] * residual[...], axis=1, keepdims=True)
    y_copy(group).wait_recv()
    zrecv[group] = own[group] + yrecv[group]

    @pl.loop(1, half)
    def _(d):
        t = group_at(half - d)
        z_copy(t, t).wait_recv()

    owned = lax.fori_loop(1, half, lambda s, total: total + zrecv[s], zrecv[0]) * w_scale
    owned_low = owned.astype(BF16)
    wall[ctr] = owned_low

    def to_mate(j, sem):
        return copy(wall.at[j], wall.at[j], sem, a_recv.at[j], "ctr", mate)

    def to_group(j, t):
        return copy(wall.at[j], wall.at[j], az_send.at[t], a_recv.at[j], "ctr", 2 * t + side)

    @pl.loop(1, half)
    def _(d):
        to_group(ctr, group_at(d)).start()

    to_mate(ctr, m_send.at[0]).start()

    w_squares = jnp.sum(owned * owned_low.astype(F32), axis=1, keepdims=True)
    lane = lax.broadcasted_iota(jnp.int32, (outputs, 128), 1)
    stats = jnp.where(
        lane == 0, w_squares, jnp.where(lane == 1, z_squares, jnp.where(lane == 2, r_squares, 0.0))
    )
    stats = jnp.concatenate([stats, jnp.zeros((128 - outputs, 128), F32)], axis=0).T[:8, :]
    stat_send[...] = stats
    stat_recv[ctr] = stats

    def s_copy(slot, peer):
        return copy(stat_send, stat_recv.at[slot], s_send.at[peer], s_recv.at[slot], "ctr", peer)

    @pl.loop(1, n_ctr)
    def _(d):
        s_copy(ctr, ctr_peer(d)).start()

    img[...] = jnp.dot(owned_low, kmat[piece_rows(ctr), :], preferred_element_type=F32)

    @pl.loop(1, half)
    def _(d):
        t = group_at(half - d)
        j = 2 * t + side
        to_group(j, t).wait_recv()
        to_mate(j, af_send.at[t]).start()
        img[...] += jnp.dot(wall[j], kmat[piece_rows(j), :], preferred_element_type=F32)

    to_mate(mate, m_send.at[0]).wait_recv()
    img[...] += jnp.dot(wall[mate], kmat[piece_rows(mate), :], preferred_element_type=F32)

    @pl.loop(1, half)
    def _(d):
        t = group_at(half - d)
        to_mate(2 * t + 1 - side, af_send.at[t]).wait_recv()

    def quarter_cols(p):
        return pl.ds(pl.multiple_of(p * quarter, quarter), quarter)

    def i_copy(p, slot):
        return copy(
            img.at[:, quarter_cols(p)], irecv.at[slot], i_send.at[p], i_recv.at[slot], "pts", p
        )

    def rest(p):
        cols = quarter_cols(p)

        @pl.loop(1, half)
        def _(d):
            j = 2 * group_at(half - d) + 1 - side
            img[:, cols] += jnp.dot(wall[j], kmat[piece_rows(j), cols], preferred_element_type=F32)

    @pl.loop(1, n_pts)
    def _(d):
        p = pts_peer(d)
        rest(p)
        i_copy(p, pts).start()

    rest(pts)
    irecv[pts] = img[:, quarter_cols(pts)]

    @pl.loop(1, n_ctr)
    def _(d):
        j = ctr_peer(n_ctr - d)
        s_copy(j, j).wait_recv()

    stat_sum = lax.fori_loop(1, n_ctr, lambda s, total: total + stat_recv[s], stat_recv[0])
    stat2_send[...] = stat_sum
    stat2_recv[pts] = stat_sum

    def t_copy(slot, peer):
        return copy(stat2_send, stat2_recv.at[slot], t_send.at[peer], t_recv.at[slot], "pts", peer)

    @pl.loop(1, n_pts)
    def _(d):
        t_copy(pts, pts_peer(d)).start()

    @pl.loop(1, n_pts)
    def _(d):
        j = pts_peer(d)
        i_copy(j, j).wait_recv()

    terms = irecv[0]
    for s in range(1, n_pts):
        terms = terms + irecv[s]
    oi[pts] = terms * image_scale + RIDGE_TERM * zvec[:, quarter_cols(pts)]

    def o_copy(slot, peer):
        return copy(oi.at[slot], oi.at[slot], o_send.at[peer], o_recv.at[slot], "pts", peer)

    @pl.loop(1, n_pts)
    def _(d):
        o_copy(pts, pts_peer(d)).start()

    for c in range(m_dev // tile_r):
        cols = slice(c * tile_r, (c + 1) * tile_r)
        prow_out[cols, :] = lax.dot_general(
            k_panel[cols, :], pinv[...], NT, preferred_element_type=F32
        ).astype(BF16)

    @pl.loop(1, n_pts)
    def _(d):
        j = pts_peer(d)
        t_copy(j, j).wait_recv()

    w_total = stat2_recv[0][0:1, :]
    for s in range(1, n_pts):
        w_total = w_total + stat2_recv[s][0:1, :]
    curvature = image_scale / w_scale * w_total + RIDGE_TERM * stat_sum[1:2, :]
    length = stat_sum[2:3, :] / curvature
    length = jnp.broadcast_to(length, (128, 128)).T[:outputs, 0:1]

    @pl.loop(1, n_pts)
    def _(d):
        j = pts_peer(d)
        o_copy(j, j).wait_recv()

    for s in range(n_pts):
        cols = slice(s * quarter, (s + 1) * quarter)
        image_out[:, cols] = oi[s]
        resid_out[:, cols] = residual[:, cols] - length * oi[s]

    @pl.when(ctr == 0)
    def _():
        @pl.loop(1, n_ctr)
        def _(d):
            vals_copy(d).wait_send()
            rows_copy(d).wait_send()

    @pl.loop(1, half)
    def _(d):
        t = group_at(d)
        y_copy(t).wait_send()
        z_copy(t, group).wait_send()
        to_group(ctr, t).wait_send()
        to_mate(2 * t + side, af_send.at[t]).wait_send()

    y_copy(group).wait_send()
    to_mate(ctr, m_send.at[0]).wait_send()

    @pl.loop(1, n_ctr)
    def _(d):
        s_copy(ctr, ctr_peer(d)).wait_send()

    @pl.loop(1, n_pts)
    def _(d):
        p = pts_peer(d)
        vals_pass(pts, p).wait_send()
        rows_pass(pts, p).wait_send()
        pin_copy(pts, p).wait_send()
        i_copy(p, pts).wait_send()
        t_copy(pts, p).wait_send()
        o_copy(pts, p).wait_send()


def relay(*refs):
    count = len(refs) // 2
    for i in range(count):
        refs[count + i][...] = refs[i][...]


def shards(n_ctr, n_pts, points, centers, panel_inverse, direction, residual):
    m_dev, features = centers.shape
    npg = points.shape[0]
    share, panel = panel_inverse.shape
    outputs = direction.shape[0]
    pieces = npg // n_ctr
    quarter = m_dev // n_pts
    half = n_ctr // 2
    vmem = pl.BlockSpec(memory_space=pltpu.VMEM)
    dma = pltpu.SemaphoreType.DMA
    ctr_sem, pts_sem, half_sem = dma((n_ctr,)), dma((n_pts,)), dma((half,))
    piece_set = pltpu.VMEM((half, outputs, pieces), F32)
    out_shape = (
        jax.ShapeDtypeStruct((m_dev, share), BF16),
        jax.ShapeDtypeStruct((outputs, m_dev), F32),
        jax.ShapeDtypeStruct((outputs, m_dev), F32),
    )
    results = pl.pallas_call(
        functools.partial(step, n_ctr, n_pts),
        out_shape=out_shape,
        in_specs=[vmem] * 5,
        out_specs=(vmem,) * 3,
        scratch_shapes=[
            pltpu.VMEM((npg, m_dev), BF16),
            pltpu.VMEM((2 * features, m_dev), BF16),
            pltpu.VMEM((n_pts, share, features), BF16),
            pltpu.VMEM((n_pts, outputs, share), BF16),
            pltpu.VMEM((n_pts, share, panel), BF16),
            pltpu.VMEM((m_dev, panel), BF16),
            pltpu.VMEM((outputs, m_dev), F32),
            pltpu.VMEM((outputs, m_dev), BF16),
            piece_set, piece_set, piece_set, piece_set,
            pltpu.VMEM((n_ctr, outputs, pieces), BF16),
            pltpu.VMEM((8, 128), F32),
            pltpu.VMEM((n_ctr, 8, 128), F32),
            pltpu.VMEM((outputs, m_dev), F32),
            pltpu.VMEM((n_pts, outputs, quarter), F32),
            pltpu.VMEM((n_pts, outputs, quarter), F32),
            pltpu.VMEM((8, 128), F32),
            pltpu.VMEM((n_pts, 8, 128), F32),
            dma((2, n_ctr)), dma((2,)), dma((2, n_pts)), dma((2, n_pts)), pts_sem, pts_sem,
            half_sem, half_sem, half_sem, half_sem, dma((1,)), half_sem, half_sem, ctr_sem,
            ctr_sem, ctr_sem, pts_sem, pts_sem, pts_sem, pts_sem, pts_sem, pts_sem,
        ],
        compiler_params=pltpu.CompilerParams(
            collective_id=0, has_side_effects=True, vmem_limit_bytes=56 * 1024 * 1024
        ),
        cost_estimate=pl.CostEstimate(
            flops=2 * npg * m_dev * (2 * features + 2 * outputs),
            bytes_accessed=4 * npg * features,
            transcendentals=npg * m_dev,
        ),
    )(points, centers, panel_inverse, direction, residual)
    return pl.pallas_call(
        relay,
        out_shape=out_shape,
        in_specs=[vmem] * 3,
        out_specs=(vmem,) * 3,
    )(*results)


def solution(mesh):
    n_ctr, n_pts = mesh.shape["ctr"], mesh.shape["pts"]
    in_specs = (P("pts", None), P("ctr", None), P("pts", None), P(None, "ctr"), P(None, "ctr"))
    out_specs = (P("ctr", "pts"), P(None, "ctr"), P(None, "ctr"))
    return jax.shard_map(
        functools.partial(shards, n_ctr, n_pts),
        mesh=mesh, in_specs=in_specs, out_specs=out_specs, check_vma=False,
    )
```

time: 89.9 us -> 68.6 us (0.76)
  Pallas kernels: 83.8 us -> 67.8 us
  local copies, waits for them, and re-layouts: 5.21 us -> 0 us
    pallas_call x1 -> x2, Pallas kernels: 83.8 us -> 67.8 us  [the longest x1 65.6 us: shards(): pl.pallas_call(functools.partial(step, n_ctr, n_pts), out_shape=out_shape...]
    unnamed x3 -> x0, local copies, waits for them, and re-layouts: 5.21 us -> none
where the time goes in v2:
time: 68.6 us; the launch traced here: 68.4 us
  Pallas kernels  67.8 us (99%)
    pallas_call x1, Pallas kernels, shards(): pl.pallas_call(functools.partial(step, n_ctr, n_pts), out_shape=out_shape...  65.6 us
    pallas_call x1, Pallas kernels, shards(): pl.pallas_call(relay, out_shape=out_shape, in_specs=[vmem] * 3, out_specs...  2.17 us

profile of v2, /device:TPU:1, one launch (start us, length us, event | category | flops | bytes accessed | tf_op | source)
XLA Modules:
  0.0 68.4 jit_solution(16709538476104345415)
XLA Ops:
  0.6 65.6 %shard_map.76 = (bf16[2048,128]{1,0:T(8,128)(2,1)}, f32[32,2048]{1,0:T(8,128)}, f32[32,2048]{1,0:T(8,128)}) custom-call(bf16[8192,128]{1,0:T(8,128)(2,1)} %points.1, bf16[2048,128]{1,0:T(8,128)(2,1)} %centers.1, bf16[128,512]{1,0:T(8,128)(2,1)} %pinv.1, f32[32,2048]{1,0:T(8,128)} %direction.1, f32[32,2048]{1,0:T(8,128)} %residual.1), custom_call_target="tpu_custom_call" | custom-call | flops 10737418240 | bytes 4194304 | tf_op jit(solution)/shard_map/pallas_call | solution.py:464
  66.3 2.2 %shard_map.77 = (bf16[2048,128]{1,0:T(8,128)(2,1)}, f32[32,2048]{1,0:T(8,128)}, f32[32,2048]{1,0:T(8,128)}) custom-call(bf16[2048,128]{1,0:T(8,128)(2,1)} %get-tuple-element.6.refs_0_, f32[32,2048]{1,0:T(8,128)} %get-tuple-element.7.refs_1_, f32[32,2048]{1,0:T(8,128)} %get-tuple-element.8.refs_2_), custom_call_target="tpu_custom_call" | custom-call | tf_op jit(solution)/shard_map/pallas_call | solution.py:500

commit v3 on v2

--- a/solution.py
+++ b/solution.py
@@ -53,7 +53,7 @@
     points, centers, pinv, direction, residual,
     prow_out, image_out, resid_out,
     kmat, right_t, head_rows, head_vals, pfull, k_panel, zvec, zlow,
-    ysend, yrecv, own, zrecv, wall, stat_send, stat_recv, img, irecv, oi, stat2_send, stat2_recv,
+    ysend, yrecv, own, zsend, zrecv, wall, stat_send, stat_recv, img, irecv, oi, stat2_send, stat2_recv,
     h_send, h_recv, g_send, g_recv, pin_send, pin_recv, y_send, y_recv, z_send, z_recv,
     m_send, az_send, af_send, a_recv,
     s_send, s_recv, i_send, i_recv, o_send, o_recv, t_send, t_recv,
@@ -163,8 +163,8 @@
                     jnp.dot(left, right_t[:, cols], preferred_element_type=F32)
                 ).astype(BF16)
 
-    early = half // 2
-    first = early // 2
+    early = max(half - half // 4, 1)
+    first = (early + 1) // 2
 
     @pl.loop(0, first)
     def _(k):
@@ -230,16 +230,16 @@
         return copy(ysend.at[t], yrecv.at[t], y_send.at[t], y_recv.at[t], "ctr", mate)
 
     def z_copy(t, slot):
-        return copy(own.at[t], zrecv.at[slot], z_send.at[t], z_recv.at[slot], "ctr", 2 * t + side)
+        return copy(zsend.at[t], zrecv.at[slot], z_send.at[t], z_recv.at[slot], "ctr", 2 * t + side)
 
     def product(t):
-        ysend[t] = partial(2 * t + 1 - side)
+        ysend[t] = partial(2 * t + 1 - side).astype(BF16)
         y_copy(t).start()
         own[t] = partial(2 * t + side)
 
     def pass_on(t):
         y_copy(t).wait_recv()
-        own[t] = own[t] + yrecv[t]
+        zsend[t] = (own[t] + yrecv[t].astype(F32)).astype(BF16)
         z_copy(t, group).start()
 
     @pl.loop(0, early)
@@ -262,14 +262,18 @@
     z_squares = jnp.sum(zvec[...] * zvec[...], axis=1, keepdims=True)
     r_squares = jnp.sum(residual[...] * residual[...], axis=1, keepdims=True)
     y_copy(group).wait_recv()
-    zrecv[group] = own[group] + yrecv[group]
 
     @pl.loop(1, half)
     def _(d):
         t = group_at(half - d)
         z_copy(t, t).wait_recv()
 
-    owned = lax.fori_loop(1, half, lambda s, total: total + zrecv[s], zrecv[0]) * w_scale
+    owned = lax.fori_loop(
+        1,
+        half,
+        lambda d, total: total + zrecv[group_at(d)].astype(F32),
+        own[group] + yrecv[group].astype(F32),
+    ) * w_scale
     owned_low = owned.astype(BF16)
     wall[ctr] = owned_low
 
@@ -456,6 +460,7 @@
     dma = pltpu.SemaphoreType.DMA
     ctr_sem, pts_sem, half_sem = dma((n_ctr,)), dma((n_pts,)), dma((half,))
     piece_set = pltpu.VMEM((half, outputs, pieces), F32)
+    sent_set = pltpu.VMEM((half, outputs, pieces), BF16)
     out_shape = (
         jax.ShapeDtypeStruct((m_dev, share), BF16),
         jax.ShapeDtypeStruct((outputs, m_dev), F32),
@@ -475,7 +480,7 @@
             pltpu.VMEM((m_dev, panel), BF16),
             pltpu.VMEM((outputs, m_dev), F32),
             pltpu.VMEM((outputs, m_dev), BF16),
-            piece_set, piece_set, piece_set, piece_set,
+            sent_set, sent_set, piece_set, sent_set, sent_set,
             pltpu.VMEM((n_ctr, outputs, pieces), BF16),
             pltpu.VMEM((8, 128), F32),
             pltpu.VMEM((n_ctr, 8, 128), F32),

time: 68.6 us -> 65 us (0.948)
  Pallas kernels: 67.8 us -> 64.2 us
    pallas_call x1, Pallas kernels: 65.6 us -> 62 us  [shards(): pl.pallas_call(functools.partial(step, n_ctr, n_pts), out_shape=out_shape...]
where the time goes in v3:
time: 65 us; the launch traced here: 64.9 us
  Pallas kernels  64.2 us (99%)
    pallas_call x1, Pallas kernels, shards(): pl.pallas_call(functools.partial(step, n_ctr, n_pts), out_shape=out_shape...  62 us
    pallas_call x1, Pallas kernels, shards(): pl.pallas_call(relay, out_shape=out_shape, in_specs=[vmem] * 3, out_specs...  2.17 us

profile of v3, /device:TPU:1, one launch (start us, length us, event | category | flops | bytes accessed | tf_op | source)
XLA Modules:
  0.0 64.9 jit_solution(14217037906136545171)
XLA Ops:
  0.6 62.0 %shard_map.76 = (bf16[2048,128]{1,0:T(8,128)(2,1)}, f32[32,2048]{1,0:T(8,128)}, f32[32,2048]{1,0:T(8,128)}) custom-call(bf16[8192,128]{1,0:T(8,128)(2,1)} %points.1, bf16[2048,128]{1,0:T(8,128)(2,1)} %centers.1, bf16[128,512]{1,0:T(8,128)(2,1)} %pinv.1, f32[32,2048]{1,0:T(8,128)} %direction.1, f32[32,2048]{1,0:T(8,128)} %residual.1), custom_call_target="tpu_custom_call" | custom-call | flops 10737418240 | bytes 4194304 | tf_op jit(solution)/shard_map/pallas_call | solution.py:469
  62.7 2.2 %shard_map.77 = (bf16[2048,128]{1,0:T(8,128)(2,1)}, f32[32,2048]{1,0:T(8,128)}, f32[32,2048]{1,0:T(8,128)}) custom-call(bf16[2048,128]{1,0:T(8,128)(2,1)} %get-tuple-element.6.refs_0_, f32[32,2048]{1,0:T(8,128)} %get-tuple-element.7.refs_1_, f32[32,2048]{1,0:T(8,128)} %get-tuple-element.8.refs_2_), custom_call_target="tpu_custom_call" | custom-call | tf_op jit(solution)/shard_map/pallas_call | solution.py:505
